TPU v7x, 128 devices: a whole 4x4x4 slice. The times are simulated.
128 devices in a mesh: blk: 64 (over y, x_lo, z, core), tower: 2 (over x_hi).
Axes of the slice: x: 4 (x_hi: 2, x_lo: 2; x = x_hi * 2 + x_lo), y: 4, z: 4, core: 2. Of those that a mesh axis runs over, the one named last changes fastest.
Arguments:
- vision_features: bfloat16 [65536, 1152], P('blk', 'tower'), may hold values from -36 to 36
- caption_features: bfloat16 [65536, 1152], P('blk', 'tower'), may hold values from -36 to 36
- sample_importance: bfloat16 [65536], P('blk'), may hold values from 0.5 to 18, as said below
- scale_exponent: float32 [1], replicated, may hold values from 2.3 to 3.4
- similarity_shift: float32 [1], replicated, may hold values from -3 to -1
Outputs:
- image_gradient: bfloat16 [65536, 1152], P('blk', 'tower')
- text_gradient: bfloat16 [65536, 1152], P('blk', 'tower')
- scalars: float32 [3], replicated
Inputs may be any that keep to these rules, and one draw needn't show every extreme that they name: `sample_importance`: positive loss weight of each pair.
All inputs are finite; a program needn't handle non-finite values.
Results may differ from a plain program's by a relative error of at most 0.012.
Values may be sent and summed in bfloat16 or wider, within the bound.
A program may use at most 64 MiB of HBM per device.

v0:
```python
import jax
import jax.numpy as jnp
from jax import lax
from jax.sharding import PartitionSpec as P

HALF = 2


def shifted(value, axis, steps):
    count = lax.axis_size(axis)
    pairs = [(source, (source + steps) % count) for source in range(count)]
    return lax.ppermute(value, axis, pairs)


def unit_rows(values):
    wide = values.astype(jnp.float32)
    row_norm = jnp.sqrt(jnp.sum(wide * wide, axis=1, keepdims=True) + 1e-06)
    return (wide / row_norm, row_norm)


def norm_gradient_backward(unit_wide, row_norm, direction):
    along = jnp.sum(unit_wide * direction, axis=1, keepdims=True)
    return ((direction - unit_wide * along) / row_norm).astype(jnp.bfloat16)


def loss_coefficients(
    image_block,
    block_weight_factor,
    text_block,
    block_offset,
    similarity_scale,
    logit_bias_value,
    diagonal_mask,
):
    cosine_matrix = lax.dot_general(
        image_block, text_block, (((1,), (1,)), ((), ())), preferred_element_type=jnp.float32
    )
    scaled_similarity = similarity_scale * cosine_matrix
    logits = scaled_similarity + logit_bias_value
    if block_offset == 0:
        losses = jax.nn.softplus(logits) - diagonal_mask * logits
        coef_wide = block_weight_factor * (jax.nn.sigmoid(logits) - diagonal_mask)
    else:
        losses = jax.nn.softplus(logits)
        coef_wide = block_weight_factor * jax.nn.sigmoid(logits)
    return (coef_wide, scaled_similarity, losses)


def shards(vision_features, caption_features, sample_importance, scale_exponent, similarity_shift):
    img_rows, txt_rows = (
        lax.all_to_all(vision_features, "tower", split_axis=0, concat_axis=1, tiled=True),
        lax.all_to_all(caption_features, "tower", split_axis=0, concat_axis=1, tiled=True),
    )
    row_count = img_rows.shape[0]
    tower_part = lax.axis_index("tower")
    weight_half = lax.dynamic_slice_in_dim(sample_importance, tower_part * row_count, row_count, 0)
    row_weight_factor = weight_half.astype(jnp.float32)[:, None]
    similarity_scale = jnp.exp(scale_exponent[0])
    logit_bias_value = similarity_shift[0]
    picture_full_vectors, picture_length = unit_rows(img_rows)
    caption_full_vectors, caption_length = unit_rows(txt_rows)
    image_unit_rows = picture_full_vectors.astype(jnp.bfloat16)
    txt_unit = caption_full_vectors.astype(jnp.bfloat16)
    diagonal_mask = (
        lax.broadcasted_iota(jnp.int32, (row_count, row_count), 0)
        == lax.broadcasted_iota(jnp.int32, (row_count, row_count), 1)
    ).astype(jnp.float32)

    def visit_block(tallies, text_block, block_offset):
        picture_running_sum, loss_sum, temp_sum, bias_sum = tallies
        coef_wide, scaled_similarity, losses = loss_coefficients(
            image_unit_rows,
            row_weight_factor,
            text_block,
            block_offset,
            similarity_scale,
            logit_bias_value,
            diagonal_mask,
        )
        coef_half = coef_wide.astype(jnp.bfloat16)
        picture_running_sum = picture_running_sum + jnp.dot(
            coef_half, text_block, preferred_element_type=jnp.float32
        )
        txt_term = None
        txt_term = lax.dot_general(
            coef_half, image_unit_rows, (((0,), (0,)), ((), ())), preferred_element_type=jnp.float32
        )
        loss_sum = loss_sum + jnp.sum(row_weight_factor * losses)
        temp_sum = temp_sum + jnp.sum(coef_wide * scaled_similarity)
        bias_sum = bias_sum + jnp.sum(coef_wide)
        return ((picture_running_sum, loss_sum, temp_sum, bias_sum), txt_term)

    zero_scalar = jnp.zeros((), jnp.float32)
    tallies = (jnp.zeros(image_unit_rows.shape, jnp.float32), zero_scalar, zero_scalar, zero_scalar)
    text_block = shifted(txt_unit, ("blk", "tower"), -HALF)
    tallies, txt_carry = visit_block(tallies, text_block, HALF)
    for advance in range(1, 2 * HALF + 1):
        text_block = shifted(text_block, ("blk", "tower"), 1)
        txt_carry = shifted(txt_carry, ("blk", "tower"), 1)
        tallies, txt_term = visit_block(tallies, text_block, HALF - advance)
        txt_carry = txt_carry + txt_term
    caption_running_sum = shifted(txt_carry.astype(jnp.bfloat16), ("blk", "tower"), -HALF).astype(
        txt_carry.dtype
    )
    picture_running_sum, loss_sum, temp_sum, bias_sum = tallies
    image_gradient = norm_gradient_backward(
        picture_full_vectors, picture_length, similarity_scale * picture_running_sum
    )
    text_gradient = norm_gradient_backward(
        caption_full_vectors, caption_length, similarity_scale * caption_running_sum
    )
    img_out, txt_out = (
        lax.all_to_all(image_gradient, "tower", split_axis=1, concat_axis=0, tiled=True),
        lax.all_to_all(text_gradient, "tower", split_axis=1, concat_axis=0, tiled=True),
    )
    loss_total, temp_total, bias_total = lax.psum((loss_sum, temp_sum, bias_sum), ("blk", "tower"))
    pair_count = row_count * lax.axis_size("blk") * lax.axis_size("tower")
    denominator = jnp.float32(pair_count * (2 * HALF + 1) * row_count)
    scalars = jnp.stack([loss_total, temp_total, bias_total]) / denominator
    return (img_out, txt_out, scalars)


def solution(mesh):
    in_specs = (P("blk", "tower"), P("blk", "tower"), P("blk"), P(), P())
    out_specs = (P("blk", "tower"), P("blk", "tower"), P())
    return jax.shard_map(shards, mesh=mesh, in_specs=in_specs, out_specs=out_specs, check_vma=False)
```

profile of v0, /device:TPU:0, one launch (start us, length us, event | category | flops | bytes accessed | tf_op | source)
XLA Modules:
  0.0 498.2 jit_solution(5400434242931149298)
XLA Ops:
  0.6 2.4 copy.38
  3.0 4.5 all-to-all-start.1
  7.5 1.1 copy.39
  8.6 15.4 %all-to-all-done.1 = bf16[2,512,576]{1,2,0:T(8,128)(2,1)S(1)} async-done(((bf16[2,512,576]{1,2,0:T(8,128)(2,1)}), bf16[2,512,576]{1,2,0:T(8,128)(2,1)S(1)}, u32[]{:S(2)}, u32[]{:S(2)}) %all-to-all-start.1) | async-done | bytes 1179680 | tf_op jit(solution)/shard_map/all_to_all | solution.py:52
  24.0 3.6 all-to-all-start
  27.6 1.7 convert_element_type.89
  29.4 2.0 copy.27
  31.4 1.6 multiply_reduce_fusion.2
  33.0 1.3 fusion.28
  34.3 5.6 %collective-permute-start = (bf16[512,1152]{1,0:T(8,128)(2,1)}, bf16[512,1152]{1,0:T(8,128)(2,1)}, u32[]{:S(2)}, u32[]{:S(2)}) collective-permute-start(bf16[512,1152]{1,0:T(8,128)(2,1)} %fusion.28), channel_id=1, source_target_pairs={{0,126},{1,127},{2,0},{3,1},{4,2},{5,3},{6,4},{7,5},{8,6},{9,7},{1... | collective-permute-start | bytes 3538952 | tf_op jit(solution)/shard_map/ppermute | solution.py:12
  41.2 0.1 dynamic-slice_convert_fusion
  41.3 1.9 all-to-all-done
  43.2 1.7 convert_element_type.88
  44.9 3.1 copy.25
  48.0 0.3 multiply_reduce_fusion.3
  48.3 1.9 fusion.27
  50.2 3.6 collective-permute-done
  53.9 2.1 convolution_multiply_fusion.4
  56.0 1.0 fusion.23
  57.0 3.9 collective-permute-start.5
  60.9 0.1 collective-permute-start.1
  61.0 81.2 %collective-permute-done.1 = bf16[512,1152]{1,0:T(8,128)(2,1)S(1)} collective-permute-done((bf16[512,1152]{1,0:T(8,128)(2,1)}, bf16[512,1152]{1,0:T(8,128)(2,1)S(1)}, u32[]{:S(2)}, u32[]{:S(2)}) %collective-permute-start.1) | collective-permute-done | bytes 1179680 | tf_op jit(solution)/shard_map/ppermute | solution.py:12
  142.2 0.9 convolution_multiply_fusion.3
  143.1 0.0 collective-permute-done.5
  143.1 1.0 convolution_add_fusion
  144.1 0.1 collective-permute-start.6
  144.2 0.1 collective-permute-start.2
  144.3 76.3 %collective-permute-done.2 = bf16[512,1152]{1,0:T(8,128)(2,1)S(1)} collective-permute-done((bf16[512,1152]{1,0:T(8,128)(2,1)S(1)}, bf16[512,1152]{1,0:T(8,128)(2,1)S(1)}, u32[]{:S(2)}, u32[]{:S(2)}) %collective-permute-start.2) | collective-permute-done | bytes 1179680 | tf_op jit(solution)/shard_map/ppermute | solution.py:12
  220.6 0.9 convolution_multiply_fusion.2
  221.5 1.0 fusion.18
  222.5 0.2 add.157
  222.7 0.1 collective-permute-start.7
  222.8 0.1 collective-permute-start.3
  222.9 2.3 fusion.25
  225.2 1.0 convolution_add_fusion.4
  226.2 75.3 %collective-permute-done.3 = bf16[512,1152]{1,0:T(8,128)(2,1)S(1)} collective-permute-done((bf16[512,1152]{1,0:T(8,128)(2,1)S(1)}, bf16[512,1152]{1,0:T(8,128)(2,1)S(1)}, u32[]{:S(2)}, u32[]{:S(2)}) %collective-permute-start.3) | collective-permute-done | bytes 1179680 | tf_op jit(solution)/shard_map/ppermute | solution.py:12
  301.5 0.0 collective-permute-start.4
  301.5 0.9 convolution_multiply_fusion.1
  302.3 1.0 fusion.15
  303.3 0.0 collective-permute-done.7
  303.3 0.2 add.158
  303.6 0.1 collective-permute-start.8
  303.7 1.0 convolution_add_fusion.3
  304.7 1.0 convolution_add_fusion.2
  305.7 51.0 %collective-permute-done.4 = bf16[512,1152]{1,0:T(8,128)(2,1)S(1)} collective-permute-done((bf16[512,1152]{1,0:T(8,128)(2,1)S(1)}, bf16[512,1152]{1,0:T(8,128)(2,1)S(1)}, u32[]{:S(2)}, u32[]{:S(2)}) %collective-permute-start.4) | collective-permute-done | bytes 1179680 | tf_op jit(solution)/shard_map/ppermute | solution.py:12
  356.6 6.3 %fusion.11 = (f32[]{:T(128)}, f32[]{:T(128)}, f32[]{:T(128)}, f32[]{:T(128)}, f32[]{:T(128)}, /*index=5*/f32[]{:T(128)}, f32[]{:T(128)}, f32[]{:T(128)}, f32[]{:...) fusion(f32[]{:T(128)} %bitcast.52, ...), kind=kOutput, calls=%fused_computation.38 | convolution fusion | flops 626524160 | bytes 7604292 | tf_op jit(solution)/shard_map/dot_general | solution.py:35
  363.0 1.0 fusion.12
  364.0 18.0 %collective-permute-done.8 = f32[512,1152]{1,0:T(8,128)S(1)} collective-permute-done((f32[512,1152]{1,0:T(8,128)S(1)}, f32[512,1152]{1,0:T(8,128)S(1)}, u32[]{:S(2)}, u32[]{:S(2)}) %collective-permute-start.8) | collective-permute-done | bytes 2359328 | tf_op jit(solution)/shard_map/ppermute | solution.py:12
  381.9 1.2 add_convert_fusion
  383.1 0.0 collective-permute-start.9
  383.1 1.3 multiply_reduce_fusion.1
  384.5 0.4 divide_convert_fusion.1
  384.9 1.4 copy.28
  386.4 4.4 all-to-all-start.2
  390.7 12.4 %collective-permute-done.9 = bf16[512,1152]{1,0:T(8,128)(2,1)} collective-permute-done((bf16[512,1152]{1,0:T(8,128)(2,1)}, bf16[512,1152]{1,0:T(8,128)(2,1)}, u32[]{:S(2)}, u32[]{:S(2)}) %collective-permute-start.9) | collective-permute-done | bytes 1179680 | tf_op jit(solution)/shard_map/ppermute | solution.py:12
  403.1 1.8 multiply_reduce_fusion
  404.9 2.8 divide_convert_fusion
  407.7 2.4 copy.30
  410.2 3.1 all-to-all-done.2
  413.3 3.6 all-to-all-start.3
  426.0 67.3 %all-reduce = (f32[1]{0:T(128)}, f32[1]{0:T(128)}, f32[1]{0:T(128)}) all-reduce(f32[1]{0:T(128)} %bitcast.12, f32[1]{0:T(128)} %bitcast.11, f32[1]{0:T(128)} %bitcast.10), channel_id=1, replica_groups=mesh['blk'=64,'tower'=2] {'blk','tower'}, use_global_device_ids=true, to_apply=%region_21.22 | all-reduce | flops 3 | bytes 24 | tf_op jit(solution)/shard_map/psum | solution.py:116
  493.3 2.5 maximum_multiply_fusion
  495.8 1.2 copy.34
  497.0 1.2 copy.35
  (12 shorter events, 0.0 us)
Async XLA Ops:
  3.0 4.5 copy-start.2
  3.0 21.0 %all-to-all-start.1 = ((bf16[2,512,576]{1,2,0:T(8,128)(2,1)}), bf16[2,512,576]{1,2,0:T(8,128)(2,1)S(1)}, u32[]{:S(2)}, u32[]{:S(2)}) async-start(bf16[2,512,576]{1,2,0:T(8,128)(2,1)} %bitcast.45), calls=%async_computation.1 | async-start | bytes 2359296 | tf_op jit(solution)/shard_map/all_to_all | solution.py:52
  24.0 3.6 copy-start.1
  24.0 19.2 %all-to-all-start = ((bf16[2,512,576]{1,2,0:T(8,128)(2,1)}), bf16[2,512,576]{1,2,0:T(8,128)(2,1)S(1)}, u32[]{:S(2)}, u32[]{:S(2)}) async-start(bf16[2,512,576]{1,2,0:T(8,128)(2,1)} %bitcast.46), calls=%async_computation | async-start | bytes 2359296 | tf_op jit(solution)/shard_map/all_to_all | solution.py:51
  33.0 8.2 %copy-start.3 = (bf16[1024]{0:T(1024)(128)(2,1)S(1)}, bf16[1024]{0:T(1024)(128)(2,1)}, u32[]{:S(2)}) copy-start(bf16[1024]{0:T(1024)(128)(2,1)} %param.7) | copy-start | bytes 6148
  34.3 19.6 %collective-permute-start = (bf16[512,1152]{1,0:T(8,128)(2,1)}, bf16[512,1152]{1,0:T(8,128)(2,1)}, u32[]{:S(2)}, u32[]{:S(2)}) collective-permute-start(bf16[512,1152]{1,0:T(8,128)(2,1)} %fusion.28), channel_id=1, source_target_pairs={{0,126},{1,127},{2,0},{3,1},{4,2},{5,3},{6,4},{7,5},{8,6},{9,7},{1... | collective-permute-start | bytes 3538952 | tf_op jit(solution)/shard_map/ppermute | solution.py:12
  57.0 86.1 %collective-permute-start.5 = (f32[512,1152]{1,0:T(8,128)S(1)}, f32[512,1152]{1,0:T(8,128)S(1)}, u32[]{:S(2)}, u32[]{:S(2)}) collective-permute-start(f32[512,1152]{1,0:T(8,128)S(1)} %fusion.23), channel_id=1, source_target_pairs={{0,1},{1,2},{2,3},{3,4},{4,5},{5,6},{6,7},{7,8},{8,9},{9,10},{10,1... | collective-permute-start | bytes 7077896 | tf_op jit(solution)/shard_map/ppermute | solution.py:12
  60.9 81.3 %collective-permute-start.1 = (bf16[512,1152]{1,0:T(8,128)(2,1)}, bf16[512,1152]{1,0:T(8,128)(2,1)S(1)}, u32[]{:S(2)}, u32[]{:S(2)}) collective-permute-start(bf16[512,1152]{1,0:T(8,128)(2,1)} %collective-permute-done), channel_id=1, source_target_pairs={{0,1},{1,2},{2,3},{3,4},{4,5},{5,6},{6,7},{7,8},{8,9},{9,10},{10,1... | collective-permute-start | bytes 3538952 | tf_op jit(solution)/shard_map/ppermute | solution.py:12
  144.1 78.4 %collective-permute-start.6 = (f32[512,1152]{1,0:T(8,128)S(1)}, f32[512,1152]{1,0:T(8,128)S(1)}, u32[]{:S(2)}, u32[]{:S(2)}) collective-permute-start(f32[512,1152]{1,0:T(8,128)S(1)} %convolution_add_fusion), channel_id=1, source_target_pairs={{0,1},{1,2},{2,3},{3,4},{4,5},{5,6},{6,7},{7,8},{8,9},{9,10},{10,1... | collective-permute-start | bytes 7077896 | tf_op jit(solution)/shard_map/ppermute | solution.py:12
  144.2 76.4 %collective-permute-start.2 = (bf16[512,1152]{1,0:T(8,128)(2,1)S(1)}, bf16[512,1152]{1,0:T(8,128)(2,1)S(1)}, u32[]{:S(2)}, u32[]{:S(2)}) collective-permute-start(bf16[512,1152]{1,0:T(8,128)(2,1)S(1)} %collective-permute-done.1), channel_id=1, source_target_pairs={{0,1},{1,2},{2,3},{3,4},{4,5},{5,6},{6,7},{7,8},{8,9},{9,10},{10,1... | collective-permute-start | bytes 3538952 | tf_op jit(solution)/shard_map/ppermute | solution.py:12
  222.7 80.6 %collective-permute-start.7 = (f32[512,1152]{1,0:T(8,128)S(1)}, f32[512,1152]{1,0:T(8,128)S(1)}, u32[]{:S(2)}, u32[]{:S(2)}) collective-permute-start(f32[512,1152]{1,0:T(8,128)S(1)} %add.157), channel_id=1, source_target_pairs={{0,1},{1,2},{2,3},{3,4},{4,5},{5,6},{6,7},{7,8},{8,9},{9,10},{10,1... | collective-permute-start | bytes 7077896 | tf_op jit(solution)/shard_map/ppermute | solution.py:12
  222.8 78.6 %collective-permute-start.3 = (bf16[512,1152]{1,0:T(8,128)(2,1)S(1)}, bf16[512,1152]{1,0:T(8,128)(2,1)S(1)}, u32[]{:S(2)}, u32[]{:S(2)}) collective-permute-start(bf16[512,1152]{1,0:T(8,128)(2,1)S(1)} %collective-permute-done.2), channel_id=1, source_target_pairs={{0,1},{1,2},{2,3},{3,4},{4,5},{5,6},{6,7},{7,8},{8,9},{9,10},{10,1... | collective-permute-start | bytes 3538952 | tf_op jit(solution)/shard_map/ppermute | solution.py:12
  301.5 55.2 %collective-permute-start.4 = (bf16[512,1152]{1,0:T(8,128)(2,1)S(1)}, bf16[512,1152]{1,0:T(8,128)(2,1)S(1)}, u32[]{:S(2)}, u32[]{:S(2)}) collective-permute-start(bf16[512,1152]{1,0:T(8,128)(2,1)S(1)} %collective-permute-done.3), channel_id=1, source_target_pairs={{0,1},{1,2},{2,3},{3,4},{4,5},{5,6},{6,7},{7,8},{8,9},{9,10},{10,1... | collective-permute-start | bytes 3538952 | tf_op jit(solution)/shard_map/ppermute | solution.py:12
  303.6 78.3 %collective-permute-start.8 = (f32[512,1152]{1,0:T(8,128)S(1)}, f32[512,1152]{1,0:T(8,128)S(1)}, u32[]{:S(2)}, u32[]{:S(2)}) collective-permute-start(f32[512,1152]{1,0:T(8,128)S(1)} %add.158), channel_id=1, source_target_pairs={{0,1},{1,2},{2,3},{3,4},{4,5},{5,6},{6,7},{7,8},{8,9},{9,10},{10,1... | collective-permute-start | bytes 7077896 | tf_op jit(solution)/shard_map/ppermute | solution.py:12
  364.0 19.2 %copy-start = (f32[512,1152]{1,0:T(8,128)S(1)}, f32[512,1152]{1,0:T(8,128)}, u32[]{:S(2)}) copy-start(f32[512,1152]{1,0:T(8,128)} %copy.25) | copy-start | bytes 7077892
  383.1 20.0 %collective-permute-start.9 = (bf16[512,1152]{1,0:T(8,128)(2,1)}, bf16[512,1152]{1,0:T(8,128)(2,1)}, u32[]{:S(2)}, u32[]{:S(2)}) collective-permute-start(bf16[512,1152]{1,0:T(8,128)(2,1)} %add_convert_fusion), channel_id=1, source_target_pairs={{0,126},{1,127},{2,0},{3,1},{4,2},{5,3},{6,4},{7,5},{8,6},{9,7},{1... | collective-permute-start | bytes 3538952 | tf_op jit(solution)/shard_map/ppermute | solution.py:12
  386.4 26.9 %all-to-all-start.2 = ((bf16[512,2,576]{0,2,1:T(8,128)(2,1)}), bf16[512,2,576]{0,2,1:T(8,128)(2,1)S(1)}, u32[]{:S(2)}, u32[]{:S(2)}) async-start(bf16[512,2,576]{0,2,1:T(8,128)(2,1)} %bitcast.62), calls=%async_computation.2 | async-start | bytes 2359296 | tf_op jit(solution)/shard_map/all_to_all | solution.py:113
  413.3 83.7 %all-to-all-start.3 = ((bf16[512,2,576]{0,2,1:T(8,128)(2,1)}), bf16[512,2,576]{0,2,1:T(8,128)(2,1)S(1)}, u32[]{:S(2)}, u32[]{:S(2)}) async-start(bf16[512,2,576]{0,2,1:T(8,128)(2,1)} %bitcast.8), calls=%async_computation.3 | async-start | bytes 2359296 | tf_op jit(solution)/shard_map/all_to_all | solution.py:114
where the time goes:
time: 500 us; the launch traced here: 498 us
  waiting for transfers between devices  338 us (68%)
  blocking collectives  67.3 us (13%)
  starting transfers between devices  26.1 us (5%)
  matrix products  22.6 us (5%)
  other arithmetic  17.9 us (4%)
  local copies, waits for them, and re-layouts  14.8 us (3%)
  between operations  11.4 us (2%)
    ppermute x10, waiting for transfers between devices, shifted(): return lax.ppermute(value, axis, pairs)  318 us
    psum x1, blocking collectives, shards(): lax.psum((loss_sum, temp_sum, bias_sum), ('blk', 'tower'))  67.3 us
    all_to_all x1, waiting for transfers between devices, shards(): lax.all_to_all(caption_features, 'tower', split_axis=0, concat_axis=1, ti...  15.4 us
    dot_general x5, matrix products, loss_coefficients(): lax.dot_general(image_block, text_block, (((1,), (1,)), ((), ())), prefer...  11.1 us
  transfers between devices with their start and end apart: 14, of which 10 were waited for; matrix products, arithmetic and copies ran while one was open for 9% of the time, Pallas kernels for 0%

commit v1 on v0

v1 whole, which is shorter than its diff:
```python
import functools
import math

import jax
import jax.numpy as jnp
from jax import lax
from jax.experimental import pallas as pl
from jax.experimental.pallas import tpu as pltpu
from jax.sharding import PartitionSpec as P

MESH = pl.DeviceIdType.MESH
F32, BF16 = jnp.float32, jnp.bfloat16
TXT, IMG = 0, 1
BLOCK = 512
SUPER = 1024
PART = 576
FULL = 1152
CHUNK = 256
CHUNKS = SUPER // CHUNK
LINE = 8
LOG2E = math.log2(math.e)


def fold(v):
    total = v[:, :128]
    for k in range(1, v.shape[1] // 128):
        total = total + v[:, 128 * k : 128 * (k + 1)]
    return total


def row_of(partial):
    return jnp.sum(jnp.transpose(partial), axis=0, keepdims=True)


def kernel(
    count,
    txt_in,
    img_in,
    weight_in,
    exponent,
    offset,
    img_out,
    txt_out,
    sums_out,
    held,
    weights,
    inv_row,
    inv_col,
    turned_txt,
    turned_img,
    txt_grad,
    txt_along,
    tallies,
    staged,
    coef,
    line_sums,
    all_sums,
    load_sem,
    x_send,
    x_recv,
    own_send,
    own_recv,
    other_send,
    other_recv,
    weight_send,
    weight_recv,
    out_sem,
    line_send,
    line_recv,
    all_send,
    all_recv,
):
    sb = lax.axis_index("blk")
    tower = lax.axis_index("tower")
    away = 1 - tower
    left, right = lax.rem(sb + count - 1, count), lax.rem(sb + 1, count)
    place, line = lax.rem(sb, LINE), sb // LINE
    lines = count // LINE
    rank = place * 2 + tower
    left_end, right_end = place == 0, place == LINE - 1
    inputs = (txt_in, img_in)
    sides = ((0, left, left_end), (1, right, right_end))

    def line_peer(k):
        there = lax.rem(rank + k, 2 * LINE)
        return there, (line * LINE + there // 2, lax.rem(there, 2))

    def all_peer(k):
        there = lax.rem(line + k, lines)
        return there, (there * LINE + place, tower)

    def columns_of(slot, c):
        return pl.ds(pl.multiple_of(slot * SUPER + c * CHUNK, CHUNK), CHUNK)

    def whole(slot):
        return pl.ds(slot * SUPER, SUPER)

    loads = []
    for a in range(2):
        target = held.at[a, pl.ds(0, PART), whole(1)]
        loads.append(pltpu.make_async_copy(inputs[a], target, load_sem.at[a]))
        loads[a].start()

    barrier = pltpu.get_barrier_semaphore()

    def greet(where):
        pl.semaphore_signal(barrier, inc=1, device_id=where, device_id_type=MESH)

    for where in ((sb, away), (left, tower), (right, tower)):
        greet(where)

    @pl.when(left_end)
    def _():
        greet((left, away))

    @pl.when(right_end)
    def _():
        greet((right, away))

    def greet_line(k, carry):
        greet(line_peer(k)[1])
        return carry

    def greet_all(k, carry):
        greet(all_peer(k)[1])
        return carry

    lax.fori_loop(1, 2 * LINE, greet_line, 0)
    lax.fori_loop(1, lines, greet_all, 0)
    at_end = jnp.logical_or(left_end, right_end)
    pl.semaphore_wait(barrier, jnp.where(at_end, 4, 3) + (2 * LINE - 1) + (lines - 1))

    def x_copy(a, c):
        return pltpu.make_async_remote_copy(
            src_ref=inputs[a].at[:, pl.ds(c * CHUNK, CHUNK)],
            dst_ref=held.at[a, pl.ds(PART, PART), columns_of(1, c)],
            send_sem=x_send.at[a, c],
            recv_sem=x_recv.at[a, c],
            device_id=(sb, away),
            device_id_type=MESH,
        )

    def own_copy(a, side):
        n, where, _ = sides[side]
        return pltpu.make_async_remote_copy(
            src_ref=inputs[a],
            dst_ref=held.at[a, pl.ds(0, PART), whole(2 - 2 * n)],
            send_sem=own_send.at[a, n],
            recv_sem=own_recv.at[a, n],
            device_id=(where, tower),
            device_id_type=MESH,
        )

    def other_copy(a, side, c):
        n, where, end = sides[side]
        first = pl.multiple_of(jnp.where(end, 0, PART), 64)
        return pltpu.make_async_remote_copy(
            src_ref=held.at[a, pl.ds(first, PART), columns_of(1, c)],
            dst_ref=held.at[a, pl.ds(PART, PART), columns_of(2 - 2 * n, c)],
            send_sem=other_send.at[a, n, c],
            recv_sem=other_recv.at[a, n, c],
            device_id=(where, jnp.where(end, away, tower)),
            device_id_type=MESH,
        )

    def weight_copy(side):
        n, where, _ = sides[side]
        return pltpu.make_async_remote_copy(
            src_ref=weights.at[1],
            dst_ref=weights.at[2 - 2 * n],
            send_sem=weight_send.at[n],
            recv_sem=weight_recv.at[n],
            device_id=(where, tower),
            device_id_type=MESH,
        )

    def line_copy(k, source):
        there, where = line_peer(k)
        return pltpu.make_async_remote_copy(
            src_ref=tallies,
            dst_ref=line_sums.at[source],
            send_sem=line_send.at[k],
            recv_sem=line_recv.at[source],
            device_id=where,
            device_id_type=MESH,
        )

    def all_copy(k, source):
        there, where = all_peer(k)
        return pltpu.make_async_remote_copy(
            src_ref=tallies,
            dst_ref=all_sums.at[source],
            send_sem=all_send.at[k],
            recv_sem=all_recv.at[source],
            device_id=where,
            device_id_type=MESH,
        )

    for a in range(2):
        for c in range(CHUNKS):
            x_copy(a, c).start()
        for side in range(2):
            own_copy(a, side).start()
    weights[1] = jnp.broadcast_to(weight_in[...].astype(F32), (8, SUPER))
    for side in range(2):
        weight_copy(side).start()

    scale = jnp.exp(jnp.full((1, 128), exponent[0], F32))[:, 0:1]
    scale2 = scale * LOG2E
    shift2 = offset[0] * LOG2E

    txt_grad[...] = jnp.zeros_like(txt_grad)
    txt_along[...] = jnp.zeros_like(txt_along)
    tallies[...] = jnp.zeros_like(tallies)
    for load in loads:
        load.wait()

    def norms(a, slot, c):
        wide = held[a, :, columns_of(slot, c)].astype(F32)
        total = jnp.sum(wide * wide, axis=0, keepdims=True)
        inverse = lax.rsqrt(total + 1e-06)
        here = pl.ds(pl.multiple_of(c * CHUNK, CHUNK), CHUNK)
        inv_row[a, slot, :, here] = jnp.broadcast_to(inverse, (8, CHUNK))
        if slot == 1:
            inv_col[a, here, :] = jnp.transpose(jnp.broadcast_to(inverse, (128, CHUNK)))

    def forward(a, c):
        x_copy(a, c).wait_recv()
        for side in range(2):
            other_copy(a, side, c).start()

    def from_sides(a, c):
        for side in range(2):

            @pl.when(c == 0)
            def _():
                own_copy(a, 1 - side).wait_recv()

            other_copy(a, 1 - side, c).wait_recv()
            norms(a, 2 * side, c)

    def text_step(c, carry):
        forward(TXT, c)
        norms(TXT, 1, c)
        here = pl.ds(pl.multiple_of(c * CHUNK, CHUNK), CHUNK)
        turned_txt[here, :] = jnp.transpose(held[TXT, :, columns_of(1, c)])
        from_sides(TXT, c)
        return carry

    lax.fori_loop(0, CHUNKS, text_step, 0)
    for side in range(2):
        weight_copy(1 - side).wait_recv()

    def image_out_copy(c):
        here = pl.ds(pl.multiple_of(c * CHUNK, CHUNK), CHUNK)
        return pltpu.make_async_copy(staged.at[IMG, :, here], img_out.at[:, here], out_sem.at[c])

    def image_rows(c):
        half = c // 2
        here = pl.ds(pl.multiple_of(c * CHUNK, CHUNK), CHUNK)
        turned_img[...] = jnp.transpose(held[IMG, :, columns_of(1, c)])
        row_scale = inv_col[IMG, here, 0:1] * scale2
        along = jnp.zeros((CHUNK, 128), F32)
        bias = jnp.zeros((CHUNK, 128), F32)
        loss = jnp.zeros((CHUNK, 128), F32)
        for j in range(5):
            begin = pl.multiple_of(half * BLOCK + j * BLOCK, BLOCK)
            slot, inside = begin // SUPER, lax.rem(begin, SUPER)
            inv_text = inv_row[TXT, slot, 0:1, pl.ds(pl.multiple_of(inside, BLOCK), BLOCK)]
            product = jnp.dot(
                turned_img[...], held[TXT, :, pl.ds(begin, BLOCK)], preferred_element_type=F32
            )
            logits2 = product * inv_text * row_scale + shift2
            grown = jnp.exp2(logits2)
            more = grown + 1.0
            sig = grown / more
            loss = loss + fold(jnp.log(more[:, :CHUNK] * more[:, CHUNK:]))
            if j == 2:
                mine = lax.broadcasted_iota(jnp.int32, (CHUNK, BLOCK), 0) + lax.rem(c, 2) * CHUNK
                match = mine == lax.broadcasted_iota(jnp.int32, (CHUNK, BLOCK), 1)
                sig = jnp.where(match, sig - 1.0, sig)
                loss = loss - fold(jnp.where(match, logits2, 0.0)) * (1.0 / LOG2E)
            scaled = sig * inv_text
            along = along + fold(scaled * product)
            bias = bias + fold(sig)
            coef[:, pl.ds(j * BLOCK, BLOCK)] = scaled.astype(BF16)
        band = pl.ds(pl.multiple_of(half * BLOCK, BLOCK), 5 * BLOCK)
        grad = lax.dot_general(
            held[TXT, pl.ds(0, PART), band],
            coef[...],
            (((1,), (1,)), ((), ())),
            preferred_element_type=F32,
        )
        weight = weights[1, 0:1, here]
        inverse = inv_row[IMG, 1, 0:1, here]
        along_row = row_of(along) * inverse
        wide = held[IMG, pl.ds(0, PART), columns_of(1, c)].astype(F32)
        result = (weight * inverse * scale) * (grad - wide * (inverse * along_row))
        staged[IMG, :, here] = result.astype(BF16)
        image_out_copy(c).start()
        for n, value in enumerate((row_of(loss), scale * along_row, row_of(bias))):
            total = jnp.sum(weight * value, axis=1, keepdims=True)
            tallies[n : n + 1, :] += jnp.broadcast_to(total, (1, 128))

    def text_rows(slot, c, block, diagonal):
        rows = pl.ds(pl.multiple_of(block * BLOCK, BLOCK), BLOCK)
        here = pl.ds(pl.multiple_of(c * CHUNK, CHUNK), CHUNK)
        there = columns_of(slot, c)
        inv_image = inv_row[IMG, slot, 0:1, here]
        heavy = inv_image * weights[slot, 0:1, here]
        row_scale = inv_col[TXT, rows, 0:1] * scale2
        product = jnp.dot(turned_txt[rows, :], held[IMG, :, there], preferred_element_type=F32)
        grown = jnp.exp2(product * inv_image * row_scale + shift2)
        sig = grown / (grown + 1.0)
        if diagonal:
            mine = lax.broadcasted_iota(jnp.int32, (BLOCK, CHUNK), 0) + block * BLOCK
            other = lax.broadcasted_iota(jnp.int32, (BLOCK, CHUNK), 1) + c * CHUNK
            sig = jnp.where(mine == other, sig - 1.0, sig)
        scaled = sig * heavy
        txt_along[rows, :] += fold(scaled * product)
        txt_grad[:, rows] += lax.dot_general(
            held[IMG, pl.ds(0, PART), there],
            scaled.astype(BF16),
            (((1,), (1,)), ((), ())),
            preferred_element_type=F32,
        )

    def image_step(c, carry):
        forward(IMG, c)
        norms(IMG, 1, c)
        image_rows(c)

        @pl.when(c == CHUNKS - 1)
        def _():
            def send(k, carry):
                line_copy(k, rank).start()
                return carry

            lax.fori_loop(1, 2 * LINE, send, 0)

        text_rows(1, c, 0, True)
        text_rows(1, c, 1, True)
        from_sides(IMG, c)
        text_rows(0, c, 0, False)
        text_rows(2, c, 1, False)
        late = c >= CHUNKS // 2
        text_rows(jnp.where(late, 0, 2), c, jnp.where(late, 1, 0), False)
        return carry

    lax.fori_loop(0, CHUNKS, image_step, 0)

    def line_wait(k, carry):
        copy = line_copy(k, line_peer(k)[0])
        copy.wait_recv()
        copy.wait_send()
        return carry

    line_sums[rank] = tallies[...]
    lax.fori_loop(1, 2 * LINE, line_wait, 0)
    total = line_sums[0]
    for k in range(1, 2 * LINE):
        total = total + line_sums[k]
    tallies[...] = total
    all_sums[line] = total

    def all_send_one(k, carry):
        all_copy(k, line).start()
        return carry

    lax.fori_loop(1, lines, all_send_one, 0)

    def text_out_copy(c):
        here = pl.ds(c * CHUNK, CHUNK)
        return pltpu.make_async_copy(
            staged.at[TXT, :, here], txt_out.at[:, here], out_sem.at[CHUNKS + c]
        )

    for c in range(CHUNKS):
        here = pl.ds(c * CHUNK, CHUNK)
        inverse = inv_row[TXT, 1, 0:1, here]
        along_row = row_of(txt_along[here, :]) * inverse
        wide = held[TXT, pl.ds(0, PART), columns_of(1, c)].astype(F32)
        result = (inverse * scale) * (txt_grad[:, here] - wide * (inverse * along_row))
        staged[TXT, :, here] = result.astype(BF16)
        text_out_copy(c).start()

    def all_wait(k, carry):
        copy = all_copy(k, all_peer(k)[0])
        copy.wait_recv()
        copy.wait_send()
        return carry

    lax.fori_loop(1, lines, all_wait, 0)
    total = all_sums[0]
    for k in range(1, lines):
        total = total + all_sums[k]
    sums_out[...] = total * (1.0 / (2.0 * count * SUPER * 5 * BLOCK))

    for c in range(CHUNKS):
        image_out_copy(c).wait()
        text_out_copy(c).wait()
    for a in range(2):
        for side in range(2):
            own_copy(a, side).wait_send()
        for c in range(CHUNKS):
            x_copy(a, c).wait_send()
            for side in range(2):
                other_copy(a, side, c).wait_send()
    for side in range(2):
        weight_copy(side).wait_send()


def shards(count, vision, caption, importance, scale_exponent, similarity_shift):
    lines = count // LINE
    dma = pltpu.SemaphoreType.DMA
    hbm, vmem = pl.BlockSpec(memory_space=pl.ANY), pl.BlockSpec(memory_space=pltpu.VMEM)
    smem = pl.BlockSpec(memory_space=pltpu.SMEM)
    img_out, txt_out, sums = pl.pallas_call(
        functools.partial(kernel, count),
        out_shape=(
            jax.ShapeDtypeStruct((PART, SUPER), BF16),
            jax.ShapeDtypeStruct((PART, SUPER), BF16),
            jax.ShapeDtypeStruct((8, 128), F32),
        ),
        in_specs=[hbm, hbm, vmem, smem, smem],
        out_specs=(hbm, hbm, vmem),
        scratch_shapes=[
            pltpu.VMEM((2, FULL, 3 * SUPER), BF16),
            pltpu.VMEM((3, 8, SUPER), F32),
            pltpu.VMEM((2, 3, 8, SUPER), F32),
            pltpu.VMEM((2, SUPER, 128), F32),
            pltpu.VMEM((SUPER, FULL), BF16),
            pltpu.VMEM((CHUNK, FULL), BF16),
            pltpu.VMEM((PART, SUPER), F32),
            pltpu.VMEM((SUPER, 128), F32),
            pltpu.VMEM((8, 128), F32),
            pltpu.VMEM((2, PART, SUPER), BF16),
            pltpu.VMEM((CHUNK, 5 * BLOCK), BF16),
            pltpu.VMEM((2 * LINE, 8, 128), F32),
            pltpu.VMEM((lines, 8, 128), F32),
            dma((2,)),
            dma((2, CHUNKS)),
            dma((2, CHUNKS)),
            dma((2, 2)),
            dma((2, 2)),
            dma((2, 2, CHUNKS)),
            dma((2, 2, CHUNKS)),
            dma((2,)),
            dma((2,)),
            dma((2 * CHUNKS,)),
            dma((2 * LINE,)),
            dma((2 * LINE,)),
            dma((lines,)),
            dma((lines,)),
        ],
        compiler_params=pltpu.CompilerParams(
            collective_id=0, has_side_effects=True, vmem_limit_bytes=60 * 2**20
        ),
        name="band",
    )(caption.T, vision.T, importance.reshape(1, SUPER), scale_exponent, similarity_shift)
    return img_out.T, txt_out.T, sums[:3, 0]


def solution(mesh):
    in_specs = (P("blk", "tower"), P("blk", "tower"), P("blk"), P(), P())
    out_specs = (P("blk", "tower"), P("blk", "tower"), P())
    return jax.shard_map(
        functools.partial(shards, mesh.shape["blk"]),
        mesh=mesh,
        in_specs=in_specs,
        out_specs=out_specs,
        check_vma=False,
    )
```

time: 500 us -> 158 us (0.32)
  waiting for transfers between devices: 338 us -> 0 us
  Pallas kernels: 0 us -> 149 us
  blocking collectives: 67.3 us -> 0 us
  starting transfers between devices: 26.1 us -> 0 us
  matrix products: 22.6 us -> 0 us
  other arithmetic: 17.9 us -> 0 us
  between operations: 11.4 us -> 1.93 us
  local copies, waits for them, and re-layouts: 14.8 us -> 6.06 us
    ppermute x10 -> x0, waiting for transfers between devices: 318 us -> none  [shifted(): return lax.ppermute(value, axis, pairs)]
    pallas_call x0 -> x1, Pallas kernels: none -> 149 us  [shards(): pl.pallas_call(functools.partial(kernel, count), out_shape=(jax.ShapeDtyp...]
    psum x1 -> x0, blocking collectives: 67.3 us -> none  [shards(): lax.psum((loss_sum, temp_sum, bias_sum), ('blk', 'tower'))]
    dot_general x15 -> x0, matrix products: 22.6 us -> none  [the longest x5 11.1 us: loss_coefficients(): lax.dot_general(image_block, text_block, (((1,), (1,)), ((), ())), prefer...]
    all_to_all x4 -> x0, waiting for transfers between devices: 20.4 us -> none  [the longest x1 15.4 us: shards(): lax.all_to_all(caption_features, 'tower', split_axis=0, concat_axis=1, ti...]
    all_to_all x4 -> x0, starting transfers between devices: 16.1 us -> none  [the longest x1 4.51 us: shards(): lax.all_to_all(caption_features, 'tower', split_axis=0, concat_axis=1, ti...]
    convert_element_type x8 -> x0, other arithmetic: 11.2 us -> none  [the longest x2 3.47 us: unit_rows(): wide = values.astype(jnp.float32)]
    ppermute x10 -> x0, starting transfers between devices: 9.99 us -> none  [shifted(): return lax.ppermute(value, axis, pairs)]
  transfers between devices with their start and end apart: 14 -> 0, of which waited for: 10 -> 0; matrix products, arithmetic and copies ran while one was open for 9% -> 0% of each run, Pallas kernels for 0% -> 0%
where the time goes in v1:
time: 158 us; the launch traced here: 157 us
  Pallas kernels  149 us (94%)
  local copies, waits for them, and re-layouts  6.06 us (4%)
  between operations  1.93 us (1%)
    pallas_call x1, Pallas kernels, shards(): pl.pallas_call(functools.partial(kernel, count), out_shape=(jax.ShapeDtyp...  149 us
    unnamed x4, local copies, waits for them, and re-layouts  3.48 us

profile of v1, /device:TPU:0, one launch (start us, length us, event | category | flops | bytes accessed | tf_op | source)
XLA Modules:
  0.0 157.3 jit_solution(14523653529949994907)
XLA Ops:
  1.9 1.3 reshape.9.weight_in
  3.2 149.3 %band.1 = (bf16[576,1024]{1,0:T(8,128)(2,1)}, bf16[576,1024]{1,0:T(8,128)(2,1)}, f32[8,128]{1,0:T(8,128)}) custom-call(bf16[576,1024]{1,0:T(8,128)(2,1)} %bitcast.4, bf16[576,1024]{1,0:T(8,128)(2,1)} %bitcast.5, bf16[1,1024]{1,0:T(2,128)(2,1)} %reshape.9.weight_in, f32[1]{0:T(128)S(6)} %copy.10.exponent, f32[1]{0:T(128)S(6)} %copy.11.offset), custom_call_target="tpu_custom_call" | custom-call | tf_op jit(solution)/shard_map/band/pallas_call | solution.py:418
  152.5 1.3 slice_reduce_fusion
  153.8 0.0 copy-start
  153.8 2.5 %copy.12 = bf16[1024,576]{0,1:T(8,128)(2,1)} copy(bf16[1024,576]{0,1:T(8,128)(2,1)} %bitcast.7) | data formatting | bytes 2359296
  156.3 0.0 copy-done
  156.3 1.0 copy.13
Async XLA Ops:
  153.8 2.5 %copy-start = (bf16[576,1024]{1,0:T(8,128)(2,1)S(1)}, bf16[576,1024]{1,0:T(8,128)(2,1)}, u32[]{:S(2)}) copy-start(bf16[576,1024]{1,0:T(8,128)(2,1)} %get-tuple-element.7) | copy-start | bytes 3538948
